TPU v7x, 32 devices: a whole 2x2x4 slice. The times are simulated.
32 devices in a mesh: parts: 2 (over x), fsdp: 8 (over z, y), tp: 2 (over core).
Axes of the slice: x: 2, y: 2, z: 4, core: 2. Of those that a mesh axis runs over, the one named last changes fastest.
Arguments:
- inputs_x: bfloat16 [256, 8192], P(('parts', 'fsdp'), 'tp'), parts along dimension 0, may hold values from -6 to 6
- out_grad: bfloat16 [256, 8192], P(('parts', 'fsdp'), 'tp'), parts along dimension 0, may hold values from -6 to 6
- w_gate: bfloat16 [8192, 14336], P(None, ('fsdp', 'tp')), may hold values from -0.0625 to 0.0625
- w_up: bfloat16 [8192, 14336], P(None, ('fsdp', 'tp')), may hold values from -0.0625 to 0.0625
- w_down: bfloat16 [8192, 14336], P(None, ('fsdp', 'tp')), may hold values from -0.046875 to 0.046875
- proj_input: bfloat16 [2, 4096, 64], P('tp', 'fsdp'), may hold values from -0.0625 to 0.0625
- proj_outgrad: bfloat16 [2, 4096, 64], P('tp', 'fsdp'), may hold values from -0.0625 to 0.0625
- proj_gate: bfloat16 [14336, 64], P(('fsdp', 'tp')), may hold values from -0.046875 to 0.046875
- proj_up: bfloat16 [14336, 64], P(('fsdp', 'tp')), may hold values from -0.046875 to 0.046875
- proj_hidden: bfloat16 [14336, 64], P(('fsdp', 'tp')), may hold values from -0.046875 to 0.046875
- index_queries: bfloat16 [8, 4096, 1536], P('fsdp', 'tp'), may hold values from -0.0546875 to 0.0546875
- block_owner: int32 [8], replicated, may hold values from 0 to 7, each once
- example_ids: int32 [16, 16], P('parts'), parts along dimension 0, may hold values from 0 to 3, never falling along the last dimension, each value on 1 to 8 neighbouring positions
Outputs:
- scores: float32 [64, 4096], P(('parts', 'fsdp'), 'tp'), parts along dimension 0
There are 2 independent parts, one for each index of `parts`. A program takes and returns all parts, laid end to end along the dimension named above; an argument that names none is the same for every part. Nothing has to cross between parts.
Inputs may be any that keep to these rules, and one draw needn't show every extreme that they name: block_owner is a permutation: index block b is held at position block_owner[b] of the first dimension of index_queries. `example_ids`: along each row the example numbers never fall.
All inputs are finite; a program needn't handle non-finite values.
Results may differ from a plain program's by a relative error of at most 0.0041.
Values may be sent and summed in bfloat16 or wider, within the bound.
A program may use at most 128 MiB of HBM per device.

v0:
```python
import jax
import jax.numpy as jnp
from jax import lax
from jax.sharding import PartitionSpec as P

EX_DEV = 4


highest_precision = lax.Precision.HIGHEST


def silu_terms(gate_pre):
    sigmoid_gate = jax.nn.sigmoid(gate_pre)
    return (gate_pre * sigmoid_gate, sigmoid_gate * (1.0 + gate_pre * (1.0 - sigmoid_gate)))


def example_grads(factors, ids, ex_count):
    rank_dim = factors.shape[-1] // 5
    a_in = factors[..., :rank_dim]
    g_out = factors[..., rank_dim : 2 * rank_dim]
    g_gate = factors[..., 2 * rank_dim : 3 * rank_dim]
    g_up = factors[..., 3 * rank_dim : 4 * rank_dim]
    a_hid = factors[..., 4 * rank_dim :]
    one_hot = (ids[:, :, None] == jnp.arange(ex_count, dtype=jnp.int32)[None, None, :]).astype(
        jnp.float32
    )

    def outer_sums(left_side, right_side):
        return jnp.einsum(
            "nte,nti,ntj->neij", one_hot, left_side, right_side, precision=highest_precision
        )

    stacked = jnp.stack(
        [outer_sums(a_in, g_gate), outer_sums(a_in, g_up), outer_sums(a_hid, g_out)], axis=2
    )
    return stacked.reshape(stacked.shape[0] * ex_count, 3 * rank_dim * rank_dim).astype(
        jnp.bfloat16
    )


def matmul(left_side, right_side):
    return jnp.dot(left_side, right_side, preferred_element_type=jnp.float32)


def layer_terms(gate_pre, up_pre, d_hidden, edge_factors, proj_gate, proj_up, proj_hidden):
    silu_gate, silu_slope = silu_terms(gate_pre)
    hidden = (silu_gate * up_pre).astype(jnp.bfloat16)
    d_gate = (d_hidden * up_pre * silu_slope).astype(jnp.bfloat16)
    d_up = (d_hidden * silu_gate).astype(jnp.bfloat16)
    return jnp.concatenate(
        [
            edge_factors,
            matmul(d_gate, proj_gate),
            matmul(d_up, proj_up),
            matmul(hidden, proj_hidden),
        ],
        axis=1,
    )


def shards(
    inputs_x,
    out_grad,
    w_gate,
    w_up,
    w_down,
    proj_input,
    proj_outgrad,
    proj_gate,
    proj_up,
    proj_hidden,
    index_queries,
    block_owner,
    example_ids,
):
    fsdp_pos = lax.axis_index("fsdp")
    core_pos = lax.axis_index("tp")
    half_width = inputs_x.shape[1]
    slice_width = proj_input.shape[1]
    stacked_rows = jnp.stack([inputs_x, out_grad], axis=1)
    p_in = proj_input[0]
    p_out = proj_outgrad[0]
    full_rows = lax.all_gather(stacked_rows, "tp", axis=2, tiled=True)
    edge_start = core_pos * half_width + fsdp_pos * slice_width
    rows_piece = lax.all_gather(full_rows, "fsdp", axis=0, tiled=True)
    x_rows = rows_piece[:, 0]
    dy_rows = rows_piece[:, 1]
    gate_pre = matmul(x_rows, w_gate)
    up_pre = matmul(x_rows, w_up)
    d_hidden = matmul(dy_rows, w_down)
    x_edge = lax.dynamic_slice_in_dim(x_rows, edge_start, slice_width, 1)
    dy_edge = lax.dynamic_slice_in_dim(dy_rows, edge_start, slice_width, 1)
    edge_factors = jnp.concatenate([matmul(x_edge, p_in), matmul(dy_edge, p_out)], axis=1)
    terms_all = layer_terms(
        gate_pre, up_pre, d_hidden, edge_factors, proj_gate, proj_up, proj_hidden
    )
    count_blocks = block_owner.shape[0]
    positions = jnp.arange(count_blocks, dtype=jnp.int32)
    own_factors = lax.psum_scatter(terms_all, ("fsdp", "tp"), scatter_dimension=0, tiled=True)
    device_factors = lax.all_gather(own_factors, "tp", axis=0, tiled=True)
    row_ids = lax.dynamic_slice_in_dim(example_ids, fsdp_pos, 1, 0)
    local_grads = example_grads(device_factors[None], row_ids, EX_DEV)
    inverse = jnp.sum(
        jnp.where(block_owner[:, None] == positions[None, :], positions[:, None], 0), axis=0
    )
    sending = jnp.take(local_grads.reshape(EX_DEV, count_blocks, -1), inverse, axis=1)
    arrived = lax.all_to_all(sending, "fsdp", split_axis=1, concat_axis=0, tiled=True)
    received = arrived.reshape(arrived.shape[0], arrived.shape[2])
    query_block = index_queries[0]
    return lax.psum_scatter(
        lax.dot_general(
            received, query_block, (((1,), (1,)), ((), ())), preferred_element_type=jnp.float32
        ),
        "fsdp",
        scatter_dimension=0,
        tiled=True,
    )


def solution(mesh):
    return jax.shard_map(
        shards,
        mesh=mesh,
        in_specs=(
            P(("parts", "fsdp"), "tp"),
            P(("parts", "fsdp"), "tp"),
            P(None, ("fsdp", "tp")),
            P(None, ("fsdp", "tp")),
            P(None, ("fsdp", "tp")),
            P("tp", "fsdp", None),
            P("tp", "fsdp", None),
            P(("fsdp", "tp"), None),
            P(("fsdp", "tp"), None),
            P(("fsdp", "tp"), None),
            P("fsdp", "tp", None),
            P(),
            P("parts", None),
        ),
        out_specs=P(("parts", "fsdp"), "tp"),
        check_vma=False,
    )
```

profile of v0, /device:TPU:0, one launch (start us, length us, event | category | flops | bytes accessed | tf_op | source)
XLA Modules:
  0.0 294.0 jit_solution(13132922714131332680)
XLA Ops:
  6.5 0.0 copy-start
  6.5 1.0 pad_maximum_fusion
  7.6 2.4 all_gather.9
  10.0 0.0 all-gather.2.cloned.1.call-update
  10.0 0.0 all-reduce.5.cloned.1.call-start
  10.0 1.2 dynamic-slice.2
  11.9 0.7 fusion.32
  12.6 0.7 select_reduce_fusion
  13.4 0.0 copy-start.4
  13.4 0.0 copy-start.5
  13.4 72.7 %all-gather.2.cloned.1.call-done = bf16[128,2,8192]{2,0,1:T(8,128)(2,1)} async-done(((bf16[16,2,8192]{2,0,1:T(8,128)(2,1)}), bf16[128,2,8192]{2,0,1:T(8,128)(2,1)}) %all-gather.2.cloned.1.call-update) | async-done | bytes 4194320 | tf_op jit(solution)/shard_map/all_gather | solution.py:85
  86.1 2.6 fusion.40
  88.8 0.0 copy-done.4
  88.8 0.0 slice-start.1
  88.8 0.8 convolution_dynamic-update-slice_fusion.4
  89.6 0.8 convolution_dynamic-update-slice_fusion.3
  90.4 0.0 slice-start.5
  90.4 0.0 slice-start.6
  90.4 9.1 %fusion.2 = f32[128,896]{1,0:T(8,128)} fusion(bf16[8192,896]{1,0:T(8,128)(2,1)} %param.15, bf16[128,2,8192]{2,0,1:T(8,128)(2,1)S(1)} %copy-done.1), kind=kOutput, calls=%fused_computation.3 | convolution fusion | flops 1879048192 | bytes 17235968 | tf_op jit(solution)/shard_map/dot_general | solution.py:42
  99.6 0.0 slice-done.1
  99.6 0.0 slice-start.7
  99.6 3.2 %fusion.4 = f32[128,896]{1,0:T(8,128)} fusion(bf16[8192,896]{1,0:T(8,128)(2,1)S(1)} %bitcast.87, bf16[128,2,8192]{2,0,1:T(8,128)(2,1)S(1)} %copy-done.1), kind=kOutput, calls=%fused_computation.5 | convolution fusion | flops 1879048192 | bytes 17235968 | tf_op jit(solution)/shard_map/dot_general | solution.py:42
  102.9 0.0 copy-start.6
  102.9 2.4 fusion.6
  105.4 0.0 copy-start.7
  105.4 0.9 convolution_dynamic-update-slice_fusion.2
  106.3 0.9 convolution_dynamic-update-slice_fusion.1
  107.2 0.9 convolution_dynamic-update-slice_fusion
  108.0 0.0 all-reduce.5.cloned.1.call-update
  108.1 0.0 all-reduce.7.cloned.1.call-start
  108.1 86.2 %all-reduce.5.cloned.1.call-done = f32[128,320]{0,1:T(8,128)} async-done(((f32[128,320]{0,1:T(8,128)}), f32[128,320]{0,1:T(8,128)}) %all-reduce.5.cloned.1.call-update) | async-done | bytes 163856
  194.3 1.0 constant_dynamic-slice_fusion.1
  195.3 0.1 copy.29
  195.4 1.9 all_gather.11
  197.2 0.5 fusion.8
  197.7 0.5 fusion.9
  198.2 0.5 fusion.10
  198.8 0.0 copy-start.8
  198.8 0.2 convert_element_type.18
  199.0 0.1 copy.31
  199.0 0.6 gather_fusion
  199.7 0.1 select_bitcast_fusion
  199.8 12.4 %all_to_all.15 = bf16[4,8,1536]{2,0,1:T(4,128)(2,1)S(1)} all-to-all(bf16[4,8,1536]{2,0,1:T(4,128)(2,1)S(1)} %select_bitcast_fusion), channel_id=1, replica_groups=mesh['parts'=2,'fsdp'=8,'tp'=2] {'fsdp'}, dimensions={1} | all-to-all | bytes 196608 | tf_op jit(solution)/shard_map/all_to_all | solution.py:107
  212.2 5.4 %fusion = f32[32,2048]{1,0:T(8,128)} fusion(bf16[32,1536]{1,0:T(8,128)(2,1)S(1)} %reshape.88, bf16[1,2048,1536]{2,1,0:T(8,128)(2,1)} %param.23), kind=kOutput, calls=%fused_computation.1 | convolution fusion | flops 201326592 | bytes 6651904 | tf_op jit(solution)/shard_map/dot_general | solution.py:111
  217.6 0.0 all-reduce.7.cloned.1.call-update
  217.7 0.6 dynamic-slice.4
  218.9 67.1 %all-reduce.7.cloned.1.call-done = f32[32,2048]{1,0:T(8,128)} async-done(((f32[32,2048]{1,0:T(8,128)}), f32[32,2048]{1,0:T(8,128)}) %all-reduce.7.cloned.1.call-update) | async-done | bytes 262160
  286.0 1.5 constant_dynamic-slice_fusion
  (33 shorter events, 0.2 us)
Async XLA Ops:
  6.5 98.8 %copy-start = (bf16[896,64]{0,1:T(8,128)(2,1)S(1)}, bf16[896,64]{0,1:T(8,128)(2,1)}, u32[]{:S(2)}) copy-start(bf16[896,64]{0,1:T(8,128)(2,1)} %param.20) | copy-start | bytes 344068
  6.5 79.6 %all-gather.2.cloned.1.call-start = ((), (), s32[]{:S(2)}) async-start(), calls=%async_computation.1 | async-start | bytes 4718592 | tf_op jit(solution)/shard_map/all_gather | solution.py:85
  10.0 184.3 %all-reduce.5.cloned.1.call-start = ((), (), s32[]{:S(2)}) async-start(), calls=%async_computation.2 | async-start | bytes 327680
  13.4 75.4 %copy-start.4 = (bf16[1,512,64]{1,2,0:T(8,128)(2,1)S(1)}, bf16[1,512,64]{1,2,0:T(8,128)(2,1)}, u32[]{:S(2)}) copy-start(bf16[1,512,64]{1,2,0:T(8,128)(2,1)} %param.18) | copy-start | bytes 196612
  13.4 76.2 %copy-start.5 = (bf16[1,512,64]{1,2,0:T(8,128)(2,1)S(1)}, bf16[1,512,64]{1,2,0:T(8,128)(2,1)}, u32[]{:S(2)}) copy-start(bf16[1,512,64]{1,2,0:T(8,128)(2,1)} %param.19) | copy-start | bytes 196612
  86.1 4.2 %copy-start.1 = (bf16[128,2,8192]{2,0,1:T(8,128)(2,1)S(1)}, bf16[128,2,8192]{2,0,1:T(8,128)(2,1)}, u32[]{:S(2)}) copy-start(bf16[128,2,8192]{2,0,1:T(8,128)(2,1)} %all-gather.2.cloned.1.call-done) | copy-start | bytes 12582916
  86.1 13.4 %slice-start = ((s8[14680064]{0:T(1024)(128)(4,1)}), s8[4194304]{0:T(1024)(128)(4,1)S(1)}, s32[]{:S(2)}) async-start(s8[14680064]{0:T(1024)(128)(4,1)} %bitcast.86), calls=%async_computation.4 | async-start | bytes 8388608
  88.8 10.8 %slice-start.1 = ((s8[14680064]{0:T(1024)(128)(4,1)}), s8[4194304]{0:T(1024)(128)(4,1)S(1)}, s32[]{:S(2)}) async-start(s8[14680064]{0:T(1024)(128)(4,1)} %bitcast.86), calls=%async_computation.5 | async-start | bytes 8388608
  90.4 9.2 %slice-start.2 = ((s8[14680064]{0:T(1024)(128)(4,1)}), s8[4194304]{0:T(1024)(128)(4,1)S(1)}, s32[]{:S(2)}) async-start(s8[14680064]{0:T(1024)(128)(4,1)} %bitcast.86), calls=%async_computation.6 | async-start | bytes 8388608
  90.4 9.2 %slice-start.3 = ((s8[14680064]{0:T(1024)(128)(4,1)}), s8[2097152]{0:T(1024)(128)(4,1)S(1)}, s32[]{:S(2)}) async-start(s8[14680064]{0:T(1024)(128)(4,1)} %bitcast.86), calls=%async_computation.7 | async-start | bytes 4194304
  90.4 12.4 %slice-start.4 = ((s8[14680064]{0:T(1024)(128)(4,1)}), s8[4194304]{0:T(1024)(128)(4,1)S(1)}, s32[]{:S(2)}) async-start(s8[14680064]{0:T(1024)(128)(4,1)} %bitcast.88), calls=%async_computation.8 | async-start | bytes 8388608
  90.4 12.4 %slice-start.5 = ((s8[14680064]{0:T(1024)(128)(4,1)}), s8[4194304]{0:T(1024)(128)(4,1)S(1)}, s32[]{:S(2)}) async-start(s8[14680064]{0:T(1024)(128)(4,1)} %bitcast.88), calls=%async_computation.9 | async-start | bytes 8388608
  90.4 12.4 %slice-start.6 = ((s8[14680064]{0:T(1024)(128)(4,1)}), s8[4194304]{0:T(1024)(128)(4,1)S(1)}, s32[]{:S(2)}) async-start(s8[14680064]{0:T(1024)(128)(4,1)} %bitcast.88), calls=%async_computation.10 | async-start | bytes 8388608
  99.6 3.2 %slice-start.7 = ((s8[14680064]{0:T(1024)(128)(4,1)}), s8[2097152]{0:T(1024)(128)(4,1)S(1)}, s32[]{:S(2)}) async-start(s8[14680064]{0:T(1024)(128)(4,1)} %bitcast.88), calls=%async_computation.11 | async-start | bytes 4194304
  102.9 2.5 copy-start.2
  102.9 2.5 copy-start.3
  102.9 3.4 %copy-start.6 = (bf16[896,64]{0,1:T(8,128)(2,1)S(1)}, bf16[896,64]{0,1:T(8,128)(2,1)}, u32[]{:S(2)}) copy-start(bf16[896,64]{0,1:T(8,128)(2,1)} %param.21) | copy-start | bytes 344068
  105.4 1.8 copy-start.7
  108.1 178.0 %all-reduce.7.cloned.1.call-start = ((), (), s32[]{:S(2)}) async-start(), calls=%async_computation.3 | async-start | bytes 524288
  198.8 18.9 %copy-start.8 = (u32[32]{0:T(128)S(1)}, u32[32]{0:T(128)}, u32[]{:S(2)}) copy-start(u32[32]{0:T(128)} %constant.45) | copy-start | bytes 388
Sparse Core Ops, SparseCore 0:
  10.1 75.9 all-gather.1
  108.2 86.0 all-reduce.4
  217.8 68.1 all-reduce.6
where the time goes:
time: 294 us
  waiting for transfers between devices  226 us (77%)
  matrix products  25.8 us (9%)
  blocking collectives  16.7 us (6%)
  between operations  14.7 us (5%)
  local copies, waits for them, and re-layouts  8.72 us (3%)
    unnamed x5, waiting for transfers between devices  153 us
    all_gather x1, waiting for transfers between devices, shards(): rows_piece = lax.all_gather(full_rows, 'fsdp', axis=0, tiled=True)  72.7 us
    dot_general x8, matrix products, matmul(): return jnp.dot(left_side, right_side, preferred_element_type=jnp.float32)  19 us
    all_to_all x1, blocking collectives, shards(): lax.all_to_all(sending, 'fsdp', split_axis=1, concat_axis=0, tiled=True)  12.4 us
  transfers between devices with their start and end apart: 3, of which 3 were waited for; matrix products, arithmetic and copies ran while one was open for 1% of the time, Pallas kernels for 0%

commit v1 on v0

--- a/solution.py
+++ b/solution.py
@@ -1,6 +1,10 @@
+import functools
+
 import jax
 import jax.numpy as jnp
 from jax import lax
+from jax.experimental import pallas as pl
+from jax.experimental.pallas import tpu as pltpu
 from jax.sharding import PartitionSpec as P
 
 EX_DEV = 4
@@ -117,9 +121,510 @@
     )
 
 
+MESH = pl.DeviceIdType.MESH
+NY = 2
+SUB = 2
+QPIECES = 4
+
+
+def dot_nt(left_side, right_side, precision=None):
+    return lax.dot_general(
+        left_side,
+        right_side,
+        (((1,), (1,)), ((), ())),
+        preferred_element_type=jnp.float32,
+        precision=precision,
+    )
+
+
+def fused_kernel(
+    n_fsdp,
+    x_hbm,
+    dy_hbm,
+    wg_hbm,
+    wu_hbm,
+    wd_hbm,
+    pin_hbm,
+    pout_hbm,
+    pg_hbm,
+    pu_hbm,
+    ph_hbm,
+    q_hbm,
+    owner_ref,
+    ids_ref,
+    out_ref,
+    rows,
+    w_vmem,
+    q_vmem,
+    pin,
+    pout,
+    pg,
+    pu,
+    ph,
+    acc,
+    fsend,
+    frecv,
+    gref,
+    gsend,
+    grecv,
+    gwide,
+    ssend,
+    srecv,
+    own_sem,
+    w_sem,
+    small_sem,
+    gather_send,
+    gather_recv,
+    sib_recv,
+    f_send_sem,
+    f_recv_sem,
+    g_send_sem,
+    g_recv_sem,
+    s_send_sem,
+    s_recv_sem,
+):
+    fs = lax.axis_index("fsdp")
+    core = lax.axis_index("tp")
+    sib = 1 - core
+    nz = n_fsdp // NY
+    z = fs // NY
+    y = lax.rem(fs, NY)
+    tok = x_hbm.shape[0]
+    wide = rows.shape[-1]
+    chunks = 2 * SUB
+    ff = wg_hbm.shape[1]
+
+    own_copies = []
+    for c in range(chunks):
+        source = x_hbm if c < SUB else dy_hbm
+        s = c % SUB
+        copy = pltpu.make_async_copy(
+            source.at[:, pl.ds(s * wide, wide)],
+            rows.at[c, core, pl.ds(fs * tok, tok), :],
+            own_sem.at[c],
+        )
+        copy.start()
+        own_copies.append(copy)
+
+    def weight_copy(matrix, hbm, s, h):
+        span = pl.ds((h * SUB + s) * wide, wide)
+        return pltpu.make_async_copy(
+            hbm.at[span, :], w_vmem.at[matrix, span, :], w_sem.at[matrix, s * 2 + h]
+        )
+
+    weights = {}
+    for s in range(SUB):
+        for h in range(2):
+            for matrix, hbm in ((0, wg_hbm), (1, wu_hbm)):
+                weights[matrix, s, h] = weight_copy(matrix, hbm, s, h)
+                weights[matrix, s, h].start()
+    small = [
+        pltpu.make_async_copy(a, b, small_sem.at[i])
+        for i, (a, b) in enumerate(
+            (
+                (pin_hbm.at[0], pin),
+                (pout_hbm.at[0], pout),
+                (pg_hbm, pg),
+                (pu_hbm, pu),
+                (ph_hbm, ph),
+                (q_hbm.at[0], q_vmem),
+            )
+        )
+    ]
+    for copy in small[:5]:
+        copy.start()
+    for s in range(SUB):
+        for h in range(2):
+            weights[2, s, h] = weight_copy(2, wd_hbm, s, h)
+            weights[2, s, h].start()
+    small[5].start()
+
+    barrier = pltpu.get_barrier_semaphore()
+    peers = [(d, t) for d in range(n_fsdp) for t in range(2) if d or t]
+    for d, t in peers:
+        pl.semaphore_signal(
+            barrier,
+            inc=1,
+            device_id={"fsdp": lax.rem(fs + d, n_fsdp), "tp": lax.rem(core + t, 2)},
+            device_id_type=MESH,
+        )
+    pl.semaphore_wait(barrier, len(peers))
+
+    UP, DOWN, ACROSS, SIB = 0, 1, 2, 3
+
+    def piece_copy(c, origin, way):
+        target_fs = {UP: fs + NY, DOWN: fs - NY, ACROSS: z * NY + (1 - y), SIB: fs}[way]
+        place = rows.at[c, core, pl.ds(origin * tok, tok), :]
+        return pltpu.make_async_remote_copy(
+            src_ref=place,
+            dst_ref=place,
+            send_sem=gather_send.at[c, way, origin],
+            recv_sem=(sib_recv if way == SIB else gather_recv).at[c, origin],
+            device_id={"fsdp": target_fs, "tp": sib if way == SIB else core},
+            device_id_type=MESH,
+        )
+
+    def wait_piece(c, origin):
+        place = rows.at[c, core, pl.ds(origin * tok, tok), :]
+        pltpu.make_async_copy(place, place, gather_recv.at[c, origin]).wait()
+
+    def send_own(c):
+        own_copies[c].wait()
+        piece_copy(c, fs, ACROSS).start()
+
+        @pl.when(z < nz - 1)
+        def _():
+            piece_copy(c, fs, UP).start()
+
+        @pl.when(z > 0)
+        def _():
+            piece_copy(c, fs, DOWN).start()
+
+        piece_copy(c, fs, SIB).start()
+
+    def forward_step(c, d):
+        if d < nz:
+
+            @pl.when(z - d >= 0)
+            def _():
+                origin = fs - d * NY
+                wait_piece(c, origin)
+
+                @pl.when(z < nz - 1)
+                def _():
+                    piece_copy(c, origin, UP).start()
+
+                piece_copy(c, origin, ACROSS).start()
+                piece_copy(c, origin, SIB).start()
+
+            @pl.when(z + d < nz)
+            def _():
+                origin = fs + d * NY
+                wait_piece(c, origin)
+
+                @pl.when(z > 0)
+                def _():
+                    piece_copy(c, origin, DOWN).start()
+
+                piece_copy(c, origin, ACROSS).start()
+                piece_copy(c, origin, SIB).start()
+
+        beside = z * NY + (1 - y)
+        back = d - 1
+
+        @pl.when(z - back >= 0)
+        def _():
+            origin = beside - back * NY
+            wait_piece(c, origin)
+            piece_copy(c, origin, SIB).start()
+
+        if back:
+
+            @pl.when(z + back < nz)
+            def _():
+                origin = beside + back * NY
+                wait_piece(c, origin)
+                piece_copy(c, origin, SIB).start()
+
+    def wait_sib(c):
+        for origin in range(n_fsdp):
+            place = rows.at[c, sib, pl.ds(origin * tok, tok), :]
+            pltpu.make_async_copy(place, place, sib_recv.at[c, origin]).wait()
+
+    def drain_sends(c):
+        for origin in range(n_fsdp):
+            oz, oy = origin // NY, origin % NY
+            piece_copy(c, origin, SIB).wait_send()
+
+            @pl.when(y == oy)
+            def _():
+                piece_copy(c, origin, ACROSS).wait_send()
+
+                @pl.when((z >= oz) & (z < nz - 1))
+                def _():
+                    piece_copy(c, origin, UP).wait_send()
+
+                @pl.when((z <= oz) & (z > 0))
+                def _():
+                    piece_copy(c, origin, DOWN).wait_send()
+
+    parts = nz
+    tile = 512
+    tiles = wide // tile
+
+    def multiply(c, part):
+        s = c % SUB
+        per = 2 // SUB if SUB > 2 else 1
+        h, rest = divmod(part, parts // 2)
+        share = tiles // (parts // 2)
+        matrices = (0, 1) if c < SUB else (2,)
+        if rest == 0:
+            for matrix in matrices:
+                weights[matrix, s, h].wait()
+
+        def body(k, carry):
+            start = pl.multiple_of((rest * share + k) * tile, tile)
+            left = rows[c, h, :, pl.ds(start, tile)]
+            for matrix in matrices:
+                base = pl.multiple_of((h * SUB + s) * wide + start, tile)
+                acc[matrix] += matmul(left, w_vmem[matrix, pl.ds(base, tile), :])
+            return carry
+
+        lax.fori_loop(0, share, body, 0)
+
+    def edge(first_chunk):
+        width = pin.shape[0]
+        per = wide // width
+        at = pl.multiple_of(lax.rem(fs, per) * width, width)
+        return rows[first_chunk + fs // per, core, :, pl.ds(at, width)]
+
+    cols = 128
+
+    def middle():
+        for copy in small[:5]:
+            copy.wait()
+        a_hid = jnp.zeros((n_fsdp * tok, ph.shape[1]), jnp.float32)
+        for n in range(ff // cols):
+            at = slice(n * cols, (n + 1) * cols)
+            gate = acc[0, :, at]
+            up = acc[1, :, at]
+            silu_gate, slope = silu_terms(gate)
+            a_hid += matmul((silu_gate * up).astype(jnp.bfloat16), ph[at, :])
+            acc[0, :, at] = up * slope
+            acc[1, :, at] = silu_gate
+        a_in = matmul(edge(0), pin[...])
+        fsend[:, 0:128] = jnp.concatenate([a_in, a_hid], axis=1).astype(jnp.bfloat16)
+
+    acc[...] = jnp.zeros_like(acc)
+    send_own(0)
+    send_own(1)
+    for c in range(chunks):
+        if c >= 1 and c + 1 < chunks:
+            send_own(c + 1)
+        for d in range(1, nz + 1):
+            forward_step(c, d)
+            if c:
+                multiply(c - 1, d - 1)
+            if c == SUB + 1 and d == 1:
+                middle()
+        wait_sib(c)
+    for part in range(parts):
+        multiply(chunks - 1, part)
+    g_out = matmul(edge(SUB), pout[...])
+    g_gate = jnp.zeros_like(g_out)
+    g_up = jnp.zeros_like(g_out)
+    for n in range(ff // cols):
+        at = slice(n * cols, (n + 1) * cols)
+        d_hidden = acc[2, :, at]
+        g_gate += matmul((d_hidden * acc[0, :, at]).astype(jnp.bfloat16), pg[at, :])
+        g_up += matmul((d_hidden * acc[1, :, at]).astype(jnp.bfloat16), pu[at, :])
+    fsend[:, 128:256] = jnp.concatenate([g_gate, g_up], axis=1).astype(jnp.bfloat16)
+    fsend[:, 256:384] = jnp.concatenate([g_out, jnp.zeros_like(g_out)], axis=1).astype(
+        jnp.bfloat16
+    )
+
+    me = fs * 2 + core
+    f_copies = []
+    for i, (d, t) in enumerate(peers):
+        target, target_core = lax.rem(fs + d, n_fsdp), lax.rem(core + t, 2)
+        copy = pltpu.make_async_remote_copy(
+            src_ref=fsend.at[pl.ds(target * tok, tok), :],
+            dst_ref=frecv.at[me],
+            send_sem=f_send_sem.at[i],
+            recv_sem=f_recv_sem.at[me],
+            device_id={"fsdp": target, "tp": target_core},
+            device_id_type=MESH,
+        )
+        copy.start()
+        f_copies.append(copy)
+    frecv[me] = fsend[pl.ds(fs * tok, tok), :]
+    for c in range(chunks):
+        drain_sends(c)
+    for d, t in peers:
+        source = lax.rem(fs + d, n_fsdp) * 2 + lax.rem(core + t, 2)
+        place = frecv.at[source]
+        pltpu.make_async_copy(place, place, f_recv_sem.at[source]).wait()
+    total = jnp.sum(frecv[...].astype(jnp.float32), axis=0)
+
+    rank = pin.shape[1]
+    pairs = rank // 2
+    a_in, a_hid = total[:, 0:64], total[:, 64:128]
+    rights = (total[:, 128:192], total[:, 192:256], total[:, 256:320])
+    row = lax.broadcasted_iota(jnp.int32, (pairs * EX_DEV, rank), 0)
+    col = lax.broadcasted_iota(jnp.int32, (pairs * EX_DEV, rank), 1)
+    token_row = lax.broadcasted_iota(jnp.int32, (pairs * EX_DEV, tok), 0)
+    ids = ids_ref[pl.ds(fs, 1), :]
+    mask = (lax.rem(token_row, EX_DEV) == ids).astype(jnp.float32)
+    picks = [(col == 2 * (row // EX_DEV) + par).astype(jnp.float32) for par in range(2)]
+    left_in = [dot_nt(pick, a_in, highest_precision) * mask for pick in picks]
+    left_hid = [dot_nt(pick, a_hid, highest_precision) * mask for pick in picks]
+    blank = jnp.zeros((tok, rank), jnp.float32)
+    for m in range(3):
+        lefts = left_hid if m == 2 else left_in
+        g = jnp.dot(
+            lefts[0],
+            jnp.concatenate([rights[m], blank], axis=1),
+            preferred_element_type=jnp.float32,
+            precision=highest_precision,
+        ) + jnp.dot(
+            lefts[1],
+            jnp.concatenate([blank, rights[m]], axis=1),
+            preferred_element_type=jnp.float32,
+            precision=highest_precision,
+        )
+        gref[pl.ds(m * pairs * EX_DEV, pairs * EX_DEV), :] = g
+
+    block_rows = gsend.shape[1]
+    for target in range(n_fsdp):
+        chosen = jnp.zeros((block_rows, 128), jnp.float32)
+        for b in range(n_fsdp):
+            keep = (owner_ref[b] == target).astype(jnp.float32)
+            chosen += keep * gref[pl.ds(b * block_rows, block_rows), :]
+        gsend[target] = chosen.astype(jnp.bfloat16)
+    g_copies = []
+    for d in range(1, n_fsdp):
+        target = lax.rem(fs + d, n_fsdp)
+        copy = pltpu.make_async_remote_copy(
+            src_ref=gsend.at[target],
+            dst_ref=grecv.at[fs],
+            send_sem=g_send_sem.at[d],
+            recv_sem=g_recv_sem.at[fs],
+            device_id={"fsdp": target, "tp": core},
+            device_id_type=MESH,
+        )
+        copy.start()
+        g_copies.append(copy)
+    grecv[fs] = gsend[fs]
+    small[5].wait()
+    for copy in f_copies:
+        copy.wait_send()
+    for d in range(1, n_fsdp):
+        source = lax.rem(fs + d, n_fsdp)
+        place = grecv.at[source]
+        pltpu.make_async_copy(place, place, g_recv_sem.at[source]).wait()
+    gwide[...] = grecv[...].astype(jnp.float32)
+    left = jnp.concatenate(
+        [
+            jnp.concatenate(
+                [gwide[f, p * EX_DEV : (p + 1) * EX_DEV, :] for f in range(n_fsdp)], axis=0
+            )
+            for p in range(block_rows // EX_DEV)
+        ],
+        axis=1,
+    ).astype(jnp.bfloat16)
+    piece = q_vmem.shape[0] // QPIECES
+    scores = [
+        dot_nt(left, q_vmem[n * piece : (n + 1) * piece, :]) for n in range(QPIECES)
+    ]
+    for f in range(n_fsdp):
+        ssend[f] = jnp.concatenate(
+            [score[f * EX_DEV : (f + 1) * EX_DEV, :] for score in scores], axis=0
+        ).astype(jnp.bfloat16)
+
+    s_copies = []
+    for d in range(1, n_fsdp):
+        target = lax.rem(fs + d, n_fsdp)
+        copy = pltpu.make_async_remote_copy(
+            src_ref=ssend.at[target],
+            dst_ref=srecv.at[fs],
+            send_sem=s_send_sem.at[d],
+            recv_sem=s_recv_sem.at[fs],
+            device_id={"fsdp": target, "tp": core},
+            device_id_type=MESH,
+        )
+        copy.start()
+        s_copies.append(copy)
+    srecv[fs] = ssend[fs]
+    for copy in g_copies:
+        copy.wait_send()
+    for d in range(1, n_fsdp):
+        source = lax.rem(fs + d, n_fsdp)
+        place = srecv.at[source]
+        pltpu.make_async_copy(place, place, s_recv_sem.at[source]).wait()
+    summed = jnp.sum(srecv[...].astype(jnp.float32), axis=0)
+    for n in range(QPIECES):
+        out_ref[:, n * piece : (n + 1) * piece] = summed[n * EX_DEV : (n + 1) * EX_DEV, :]
+    for copy in s_copies:
+        copy.wait_send()
+
+
+def fused_shards(n_fsdp, *args):
+    x, _, wg = args[:3]
+    pin, pg = args[5], args[7]
+    q = args[10]
+    tok, half = x.shape
+    tokens = n_fsdp * tok
+    wide = half // SUB
+    depth, ff = wg.shape
+    rank = pg.shape[1]
+    queries, block = q.shape[1:]
+    chunks = 2 * SUB
+    block_rows = block // 128 * EX_DEV
+    dma = pltpu.SemaphoreType.DMA
+    bf16, f32 = jnp.bfloat16, jnp.float32
+    hbm = pl.BlockSpec(memory_space=pl.ANY)
+    return pl.pallas_call(
+        functools.partial(fused_kernel, n_fsdp),
+        out_shape=jax.ShapeDtypeStruct((EX_DEV, queries), f32),
+        in_specs=[hbm] * 11
+        + [pl.BlockSpec(memory_space=pltpu.SMEM), pl.BlockSpec(memory_space=pltpu.VMEM)],
+        out_specs=pl.BlockSpec(memory_space=pltpu.VMEM),
+        scratch_shapes=[
+            pltpu.VMEM((chunks, 2, tokens, wide), bf16),
+            pltpu.VMEM((3, depth, ff), bf16),
+            pltpu.VMEM((queries, block), bf16),
+            pltpu.VMEM(pin.shape[1:], bf16),
+            pltpu.VMEM(pin.shape[1:], bf16),
+            pltpu.VMEM((ff, rank), bf16),
+            pltpu.VMEM((ff, rank), bf16),
+            pltpu.VMEM((ff, rank), bf16),
+            pltpu.VMEM((3, tokens, ff), f32),
+            pltpu.VMEM((tokens, 6 * rank), bf16),
+            pltpu.VMEM((2 * n_fsdp, tok, 6 * rank), bf16),
+            pltpu.VMEM((n_fsdp * block_rows, 128), f32),
+            pltpu.VMEM((n_fsdp, block_rows, 128), bf16),
+            pltpu.VMEM((n_fsdp, block_rows, 128), bf16),
+            pltpu.VMEM((n_fsdp, block_rows, 128), f32),
+            pltpu.VMEM((n_fsdp, QPIECES * EX_DEV, queries // QPIECES), bf16),
+            pltpu.VMEM((n_fsdp, QPIECES * EX_DEV, queries // QPIECES), bf16),
+            dma((chunks,)),
+            dma((3, 2 * SUB)),
+            dma((6,)),
+            dma((chunks, 4, n_fsdp)),
+            dma((chunks, n_fsdp)),
+            dma((chunks, n_fsdp)),
+            dma((2 * n_fsdp,)),
+            dma((2 * n_fsdp,)),
+            dma((n_fsdp,)),
+            dma((n_fsdp,)),
+            dma((n_fsdp,)),
+            dma((n_fsdp,)),
+        ],
+        compiler_params=pltpu.CompilerParams(
+            collective_id=0, has_side_effects=True, vmem_limit_bytes=62 * 1024 * 1024
+        ),
+    )(*args)
+
+
+def pick_shards(n_fsdp, n_tp):
+    def run(*args):
+        x, wg, q = args[0], args[2], args[10]
+        fits = (
+            n_tp == 2
+            and n_fsdp == 8
+            and x.shape[0] == 16
+            and args[7].shape[1] == 64
+            and wg.shape[1] % 128 == 0
+            and wg.size * 6 + q.size * 2 < 52 * 1024 * 1024
+        )
+        return fused_shards(n_fsdp, *args) if fits else shards(*args)
+
+    return run
+
+
 def solution(mesh):
     return jax.shard_map(
-        shards,
+        pick_shards(mesh.shape["fsdp"], mesh.shape["tp"]),
         mesh=mesh,
         in_specs=(
             P(("parts", "fsdp"), "tp"),

time: 294 us -> 91.1 us (0.31)
  waiting for transfers between devices: 226 us -> 0 us
  Pallas kernels: 0 us -> 81 us
  matrix products: 25.8 us -> 0 us
  blocking collectives: 16.7 us -> 0 us
  between operations: 14.7 us -> 0.01 us
    unnamed x5 -> x0, waiting for transfers between devices: 153 us -> none
    pallas_call x0 -> x1, Pallas kernels: none -> 81 us  [fused_shards(): pl.pallas_call(functools.partial(fused_kernel, n_fsdp), out_shape=jax.Sha...]
    all_gather x1 -> x0, waiting for transfers between devices: 72.7 us -> none  [shards(): rows_piece = lax.all_gather(full_rows, 'fsdp', axis=0, tiled=True)]
    dot_general x12 -> x0, matrix products: 25.8 us -> none  [the longest x8 19 us: matmul(): return jnp.dot(left_side, right_side, preferred_element_type=jnp.float32)]
    all_to_all x1 -> x0, blocking collectives: 12.4 us -> none  [shards(): lax.all_to_all(sending, 'fsdp', split_axis=1, concat_axis=0, tiled=True)]
    unnamed x38 -> x6, local copies, waits for them, and re-layouts: 4.39 us -> 9.72 us
    all_gather x2 -> x0, blocking collectives: 4.27 us -> none  [the longest x1 2.39 us: shards(): full_rows = lax.all_gather(stacked_rows, 'tp', axis=2, tiled=True)]
  transfers between devices with their start and end apart: 3 -> 0, of which waited for: 3 -> 0; matrix products, arithmetic and copies ran while one was open for 1% -> 0% of each run, Pallas kernels for 0% -> 0%
where the time goes in v1:
time: 91.1 us; the launch traced here: 90.7 us
  Pallas kernels  81 us (89%)
  local copies, waits for them, and re-layouts  9.72 us (11%)
    pallas_call x1, Pallas kernels, fused_shards(): pl.pallas_call(functools.partial(fused_kernel, n_fsdp), out_shape=jax.Sha...  81 us
    unnamed x6, local copies, waits for them, and re-layouts  9.72 us

profile of v1, /device:TPU:0, one launch (start us, length us, event | category | flops | bytes accessed | tf_op | source)
XLA Modules:
  0.0 90.7 jit_solution(10273291919966528020)
XLA Ops:
  0.0 1.6 %copy.14.pin_hbm = bf16[1,512,64]{2,1,0:T(8,128)(2,1)} copy(bf16[1,512,64]{1,2,0:T(8,128)(2,1)} %param.18) | data formatting | bytes 131072 | tf_op args[5]
  1.6 1.6 %copy.15.pout_hbm = bf16[1,512,64]{2,1,0:T(8,128)(2,1)} copy(bf16[1,512,64]{1,2,0:T(8,128)(2,1)} %param.19) | data formatting | bytes 131072 | tf_op args[6]
  3.2 1.7 %copy.16.pg_hbm = bf16[896,64]{1,0:T(8,128)(2,1)} copy(bf16[896,64]{0,1:T(8,128)(2,1)} %param.20) | data formatting | bytes 229376 | tf_op args[7]
  4.9 1.7 %copy.17.pu_hbm = bf16[896,64]{1,0:T(8,128)(2,1)} copy(bf16[896,64]{0,1:T(8,128)(2,1)} %param.21) | data formatting | bytes 229376 | tf_op args[8]
  6.6 1.7 %copy.18.ph_hbm = bf16[896,64]{1,0:T(8,128)(2,1)} copy(bf16[896,64]{0,1:T(8,128)(2,1)} %param.22) | data formatting | bytes 229376 | tf_op args[9]
  8.3 81.0 %shard_map.127 = f32[4,2048]{1,0:T(4,128)} custom-call(bf16[16,4096]{1,0:T(8,128)(2,1)} %x_hbm.1, bf16[16,4096]{1,0:T(8,128)(2,1)} %dy_hbm.1, bf16[8192,896]{1,0:T(8,128)(2,1)} %wg_hbm.1, bf16[8192,896]{1,0:T(8,128)(2,1)} %wu_hbm.1, bf16[8192,896]{1,0:T(8,128)(2,1)} %wd_hbm.1, bf16[1,512,64]{2,1,0:T(8,128)(2,1)} %copy.14.pin_hbm, ...), custom_call_target="tpu_custom_call" | custom-call | tf_op jit(solution)/shard_map/pallas_call | solution.py:566
  89.3 1.4 %copy.20 = f32[4,2048]{1,0:T(4,128)} copy(f32[4,2048]{1,0:T(4,128)} %shard_map.127) | data formatting | bytes 65536

commit v2 on v1

--- a/solution.py
+++ b/solution.py
@@ -162,8 +162,12 @@
     pu,
     ph,
     acc,
-    fsend,
-    frecv,
+    early_send,
+    early_recv,
+    late_send,
+    late_recv,
+    pair_send,
+    pair_recv,
     gref,
     gsend,
     grecv,
@@ -178,6 +182,7 @@
     sib_recv,
     f_send_sem,
     f_recv_sem,
+    pair_sem,
     g_send_sem,
     g_recv_sem,
     s_send_sem,
@@ -222,8 +227,8 @@
         pltpu.make_async_copy(a, b, small_sem.at[i])
         for i, (a, b) in enumerate(
             (
-                (pin_hbm.at[0], pin),
-                (pout_hbm.at[0], pout),
+                (pin_hbm, pin),
+                (pout_hbm, pout),
                 (pg_hbm, pg),
                 (pu_hbm, pu),
                 (ph_hbm, ph),
@@ -373,27 +378,51 @@
         lax.fori_loop(0, share, body, 0)
 
     def edge(first_chunk):
-        width = pin.shape[0]
+        width = pin.shape[1]
         per = wide // width
         at = pl.multiple_of(lax.rem(fs, per) * width, width)
         return rows[first_chunk + fs // per, core, :, pl.ds(at, width)]
 
+    f_copies = []
+
+    def send_factors(src, dst, stage):
+        for d in range(1, n_fsdp):
+            target = lax.rem(fs + d, n_fsdp)
+            copy = pltpu.make_async_remote_copy(
+                src_ref=src.at[pl.ds(target * tok, tok), :],
+                dst_ref=dst.at[fs],
+                send_sem=f_send_sem.at[stage, d],
+                recv_sem=f_recv_sem.at[stage, fs],
+                device_id={"fsdp": target, "tp": core},
+                device_id_type=MESH,
+            )
+            copy.start()
+            f_copies.append(copy)
+        dst[fs] = src[pl.ds(fs * tok, tok), :]
+
+    def arrive_factors(dst, stage):
+        for d in range(1, n_fsdp):
+            source = lax.rem(fs + d, n_fsdp)
+            place = dst.at[source]
+            pltpu.make_async_copy(place, place, f_recv_sem.at[stage, source]).wait()
+
     cols = 128
 
     def middle():
         for copy in small[:5]:
             copy.wait()
-        a_hid = jnp.zeros((n_fsdp * tok, ph.shape[1]), jnp.float32)
+        a_hid = jnp.zeros((n_fsdp * tok, ph.shape[0]), jnp.float32)
         for n in range(ff // cols):
             at = slice(n * cols, (n + 1) * cols)
             gate = acc[0, :, at]
             up = acc[1, :, at]
             silu_gate, slope = silu_terms(gate)
-            a_hid += matmul((silu_gate * up).astype(jnp.bfloat16), ph[at, :])
+            a_hid += dot_nt((silu_gate * up).astype(jnp.bfloat16), ph[:, at])
             acc[0, :, at] = up * slope
             acc[1, :, at] = silu_gate
-        a_in = matmul(edge(0), pin[...])
-        fsend[:, 0:128] = jnp.concatenate([a_in, a_hid], axis=1).astype(jnp.bfloat16)
+        a_in = dot_nt(edge(0), pin[...])
+        early_send[...] = jnp.concatenate([a_in, a_hid], axis=1)
+        send_factors(early_send, early_recv, 0)
 
     acc[...] = jnp.zeros_like(acc)
     send_own(0)
@@ -410,43 +439,37 @@
         wait_sib(c)
     for part in range(parts):
         multiply(chunks - 1, part)
-    g_out = matmul(edge(SUB), pout[...])
+    g_out = dot_nt(edge(SUB), pout[...])
     g_gate = jnp.zeros_like(g_out)
     g_up = jnp.zeros_like(g_out)
     for n in range(ff // cols):
         at = slice(n * cols, (n + 1) * cols)
         d_hidden = acc[2, :, at]
-        g_gate += matmul((d_hidden * acc[0, :, at]).astype(jnp.bfloat16), pg[at, :])
-        g_up += matmul((d_hidden * acc[1, :, at]).astype(jnp.bfloat16), pu[at, :])
-    fsend[:, 128:256] = jnp.concatenate([g_gate, g_up], axis=1).astype(jnp.bfloat16)
-    fsend[:, 256:384] = jnp.concatenate([g_out, jnp.zeros_like(g_out)], axis=1).astype(
-        jnp.bfloat16
-    )
-
-    me = fs * 2 + core
-    f_copies = []
-    for i, (d, t) in enumerate(peers):
-        target, target_core = lax.rem(fs + d, n_fsdp), lax.rem(core + t, 2)
-        copy = pltpu.make_async_remote_copy(
-            src_ref=fsend.at[pl.ds(target * tok, tok), :],
-            dst_ref=frecv.at[me],
-            send_sem=f_send_sem.at[i],
-            recv_sem=f_recv_sem.at[me],
-            device_id={"fsdp": target, "tp": target_core},
-            device_id_type=MESH,
-        )
-        copy.start()
-        f_copies.append(copy)
-    frecv[me] = fsend[pl.ds(fs * tok, tok), :]
+        g_gate += dot_nt((d_hidden * acc[0, :, at]).astype(jnp.bfloat16), pg[:, at])
+        g_up += dot_nt((d_hidden * acc[1, :, at]).astype(jnp.bfloat16), pu[:, at])
+    late_send[:, 0:128] = jnp.concatenate([g_gate, g_up], axis=1)
+    late_send[:, 128:256] = jnp.concatenate([g_out, jnp.zeros_like(g_out)], axis=1)
+
+    send_factors(late_send, late_recv, 1)
     for c in range(chunks):
         drain_sends(c)
-    for d, t in peers:
-        source = lax.rem(fs + d, n_fsdp) * 2 + lax.rem(core + t, 2)
-        place = frecv.at[source]
-        pltpu.make_async_copy(place, place, f_recv_sem.at[source]).wait()
-    total = jnp.sum(frecv[...].astype(jnp.float32), axis=0)
-
-    rank = pin.shape[1]
+    arrive_factors(early_recv, 0)
+    pair_send[:, 0:128] = jnp.sum(early_recv[...], axis=0)
+    arrive_factors(late_recv, 1)
+    pair_send[:, 128:384] = jnp.sum(late_recv[...], axis=0)
+    pair_copy = pltpu.make_async_remote_copy(
+        src_ref=pair_send,
+        dst_ref=pair_recv,
+        send_sem=pair_sem.at[0],
+        recv_sem=pair_sem.at[1],
+        device_id={"fsdp": fs, "tp": sib},
+        device_id_type=MESH,
+    )
+    pair_copy.start()
+    pair_copy.wait_recv()
+    total = pair_send[...] + pair_recv[...]
+
+    rank = pin.shape[0]
     pairs = rank // 2
     a_in, a_hid = total[:, 0:64], total[:, 64:128]
     rights = (total[:, 128:192], total[:, 192:256], total[:, 256:320])
@@ -498,6 +521,7 @@
     small[5].wait()
     for copy in f_copies:
         copy.wait_send()
+    pair_copy.wait_send()
     for d in range(1, n_fsdp):
         source = lax.rem(fs + d, n_fsdp)
         place = grecv.at[source]
@@ -550,13 +574,14 @@
 
 def fused_shards(n_fsdp, *args):
     x, _, wg = args[:3]
-    pin, pg = args[5], args[7]
+    flat = [a[0].T for a in args[5:7]] + [a.T for a in args[7:10]]
+    pin = flat[0]
     q = args[10]
     tok, half = x.shape
     tokens = n_fsdp * tok
     wide = half // SUB
     depth, ff = wg.shape
-    rank = pg.shape[1]
+    rank = pin.shape[0]
     queries, block = q.shape[1:]
     chunks = 2 * SUB
     block_rows = block // 128 * EX_DEV
@@ -573,14 +598,18 @@
             pltpu.VMEM((chunks, 2, tokens, wide), bf16),
             pltpu.VMEM((3, depth, ff), bf16),
             pltpu.VMEM((queries, block), bf16),
-            pltpu.VMEM(pin.shape[1:], bf16),
-            pltpu.VMEM(pin.shape[1:], bf16),
-            pltpu.VMEM((ff, rank), bf16),
-            pltpu.VMEM((ff, rank), bf16),
-            pltpu.VMEM((ff, rank), bf16),
+            pltpu.VMEM(pin.shape, bf16),
+            pltpu.VMEM(pin.shape, bf16),
+            pltpu.VMEM((rank, ff), bf16),
+            pltpu.VMEM((rank, ff), bf16),
+            pltpu.VMEM((rank, ff), bf16),
             pltpu.VMEM((3, tokens, ff), f32),
-            pltpu.VMEM((tokens, 6 * rank), bf16),
-            pltpu.VMEM((2 * n_fsdp, tok, 6 * rank), bf16),
+            pltpu.VMEM((tokens, 2 * rank), f32),
+            pltpu.VMEM((n_fsdp, tok, 2 * rank), f32),
+            pltpu.VMEM((tokens, 4 * rank), f32),
+            pltpu.VMEM((n_fsdp, tok, 4 * rank), f32),
+            pltpu.VMEM((tok, 6 * rank), f32),
+            pltpu.VMEM((tok, 6 * rank), f32),
             pltpu.VMEM((n_fsdp * block_rows, 128), f32),
             pltpu.VMEM((n_fsdp, block_rows, 128), bf16),
             pltpu.VMEM((n_fsdp, block_rows, 128), bf16),
@@ -593,8 +622,9 @@
             dma((chunks, 4, n_fsdp)),
             dma((chunks, n_fsdp)),
             dma((chunks, n_fsdp)),
-            dma((2 * n_fsdp,)),
-            dma((2 * n_fsdp,)),
+            dma((2, n_fsdp)),
+            dma((2, n_fsdp)),
+            dma((2,)),
             dma((n_fsdp,)),
             dma((n_fsdp,)),
             dma((n_fsdp,)),
@@ -603,7 +633,7 @@
         compiler_params=pltpu.CompilerParams(
             collective_id=0, has_side_effects=True, vmem_limit_bytes=62 * 1024 * 1024
         ),
-    )(*args)
+    )(*args[:5], *flat, *args[10:])
 
 
 def pick_shards(n_fsdp, n_tp):

time: 91.1 us -> 83.1 us (0.912)
  local copies, waits for them, and re-layouts: 9.72 us -> 1.38 us
    unnamed x6 -> x1, local copies, waits for them, and re-layouts: 9.72 us -> 1.38 us
where the time goes in v2:
time: 83.1 us; the launch traced here: 82.9 us
  Pallas kernels  81.5 us (98%)
  local copies, waits for them, and re-layouts  1.38 us (2%)
    pallas_call x1, Pallas kernels, fused_shards(): pl.pallas_call(functools.partial(fused_kernel, n_fsdp), out_shape=jax.Sha...  81.5 us

profile of v2, /device:TPU:0, one launch (start us, length us, event | category | flops | bytes accessed | tf_op | source)
XLA Modules:
  0.0 82.9 jit_solution(16657319604787918023)
XLA Ops:
  0.0 81.5 %shard_map.127 = f32[4,2048]{1,0:T(4,128)} custom-call(bf16[16,4096]{1,0:T(8,128)(2,1)} %x_hbm.1, bf16[16,4096]{1,0:T(8,128)(2,1)} %dy_hbm.1, bf16[8192,896]{1,0:T(8,128)(2,1)} %wg_hbm.1, bf16[8192,896]{1,0:T(8,128)(2,1)} %wu_hbm.1, bf16[8192,896]{1,0:T(8,128)(2,1)} %wd_hbm.1, bf16[64,512]{1,0:T(8,128)(2,1)} %bitcast.12, bf16[64,512]{1,0:T(8,128)(2,1)} %bitcast.13, ...), custom_call_target="tpu_custom_call" | custom-call | tf_op jit(solution)/shard_map/pallas_call | solution.py:591
  81.5 1.4 %copy.15 = f32[4,2048]{1,0:T(4,128)} copy(f32[4,2048]{1,0:T(4,128)} %shard_map.127) | data formatting | bytes 65536

commit v3 on v2

--- a/solution.py
+++ b/solution.py
@@ -125,6 +125,9 @@
 NY = 2
 SUB = 2
 QPIECES = 4
+SKEW = 1
+LAG = 1
+PER = 1
 
 
 def dot_nt(left_side, right_side, precision=None):
@@ -273,6 +276,13 @@
         place = rows.at[c, core, pl.ds(origin * tok, tok), :]
         pltpu.make_async_copy(place, place, gather_recv.at[c, origin]).wait()
 
+    def goes_across(c, at, origin_z):
+        if c % 2 == 0:
+            return at >= 0
+        low = (origin_z == 0) & ((at == 1) | (at == nz - 1))
+        high = (origin_z == nz - 1) & ((at == nz - 2) | (at == 0))
+        return jnp.logical_not(low | high)
+
     def send_own(c):
         own_copies[c].wait()
         piece_copy(c, fs, ACROSS).start()
@@ -299,7 +309,10 @@
                 def _():
                     piece_copy(c, origin, UP).start()
 
-                piece_copy(c, origin, ACROSS).start()
+                @pl.when(goes_across(c, z, z - d))
+                def _():
+                    piece_copy(c, origin, ACROSS).start()
+
                 piece_copy(c, origin, SIB).start()
 
             @pl.when(z + d < nz)
@@ -311,7 +324,10 @@
                 def _():
                     piece_copy(c, origin, DOWN).start()
 
-                piece_copy(c, origin, ACROSS).start()
+                @pl.when(goes_across(c, z, z + d))
+                def _():
+                    piece_copy(c, origin, ACROSS).start()
+
                 piece_copy(c, origin, SIB).start()
 
         beside = z * NY + (1 - y)
@@ -321,6 +337,18 @@
         def _():
             origin = beside - back * NY
             wait_piece(c, origin)
+            if c % 2 and back in (0, nz - 2):
+
+                @pl.when(z == back)
+                def _():
+                    piece_copy(c, origin, UP).start()
+
+            if c % 2 and back == 0:
+
+                @pl.when(z == nz - 1)
+                def _():
+                    piece_copy(c, origin, DOWN).start()
+
             piece_copy(c, origin, SIB).start()
 
         if back:
@@ -329,6 +357,12 @@
             def _():
                 origin = beside + back * NY
                 wait_piece(c, origin)
+                if c % 2 and back == nz - 2:
+
+                    @pl.when(z == 1)
+                    def _():
+                        piece_copy(c, origin, DOWN).start()
+
                 piece_copy(c, origin, SIB).start()
 
     def wait_sib(c):
@@ -343,13 +377,28 @@
 
             @pl.when(y == oy)
             def _():
-                piece_copy(c, origin, ACROSS).wait_send()
+
+                @pl.when(goes_across(c, z, oz))
+                def _():
+                    piece_copy(c, origin, ACROSS).wait_send()
 
                 @pl.when((z >= oz) & (z < nz - 1))
                 def _():
                     piece_copy(c, origin, UP).wait_send()
 
                 @pl.when((z <= oz) & (z > 0))
+                def _():
+                    piece_copy(c, origin, DOWN).wait_send()
+
+            if c % 2 and oz == 0:
+
+                @pl.when((y != oy) & ((z == 0) | (z == nz - 2)))
+                def _():
+                    piece_copy(c, origin, UP).wait_send()
+
+            if c % 2 and oz == nz - 1:
+
+                @pl.when((y != oy) & ((z == nz - 1) | (z == 1)))
                 def _():
                     piece_copy(c, origin, DOWN).wait_send()
 
@@ -424,21 +473,35 @@
         early_send[...] = jnp.concatenate([a_in, a_hid], axis=1)
         send_factors(early_send, early_recv, 0)
 
+    def run_unit(c, part):
+        if part == 0:
+            wait_sib(c)
+        multiply(c, part)
+        if c == SUB - 1 and part == parts - 1:
+            middle()
+
     acc[...] = jnp.zeros_like(acc)
-    send_own(0)
-    send_own(1)
     for c in range(chunks):
-        if c >= 1 and c + 1 < chunks:
-            send_own(c + 1)
-        for d in range(1, nz + 1):
-            forward_step(c, d)
-            if c:
-                multiply(c - 1, d - 1)
-            if c == SUB + 1 and d == 1:
-                middle()
-        wait_sib(c)
-    for part in range(parts):
-        multiply(chunks - 1, part)
+        send_own(c)
+    order = sorted(
+        (d + SKEW * c, c, d) for c in range(chunks) for d in range(1, nz + 1)
+    )
+    ready = []
+    work = []
+    for _, c, d in order:
+        ready.append((c, d))
+        forward_step(c, d)
+        if len(ready) > LAG and ready[-1 - LAG][1] == nz:
+            done = ready[-1 - LAG][0]
+            work += [(done, part) for part in range(parts)]
+        for _ in range(PER):
+            if work:
+                run_unit(*work.pop(0))
+    for c, d in ready[-LAG:]:
+        if d == nz:
+            work += [(c, part) for part in range(parts)]
+    for unit in work:
+        run_unit(*unit)
     g_out = dot_nt(edge(SUB), pout[...])
     g_gate = jnp.zeros_like(g_out)
     g_up = jnp.zeros_like(g_out)

time: 83.1 us -> 71.3 us (0.86)
  Pallas kernels: 81.5 us -> 69.8 us
    pallas_call x1, Pallas kernels: 81.5 us -> 69.8 us  [fused_shards(): pl.pallas_call(functools.partial(fused_kernel, n_fsdp), out_shape=jax.Sha...]
where the time goes in v3:
time: 71.3 us; the launch traced here: 71.1 us
  Pallas kernels  69.8 us (98%)
  local copies, waits for them, and re-layouts  1.38 us (2%)
    pallas_call x1, Pallas kernels, fused_shards(): pl.pallas_call(functools.partial(fused_kernel, n_fsdp), out_shape=jax.Sha...  69.8 us

profile of v3, /device:TPU:0, one launch (start us, length us, event | category | flops | bytes accessed | tf_op | source)
XLA Modules:
  0.0 71.1 jit_solution(4878939661869458673)
XLA Ops:
  0.0 69.8 %shard_map.127 = f32[4,2048]{1,0:T(4,128)} custom-call(bf16[16,4096]{1,0:T(8,128)(2,1)} %x_hbm.1, bf16[16,4096]{1,0:T(8,128)(2,1)} %dy_hbm.1, bf16[8192,896]{1,0:T(8,128)(2,1)} %wg_hbm.1, bf16[8192,896]{1,0:T(8,128)(2,1)} %wu_hbm.1, bf16[8192,896]{1,0:T(8,128)(2,1)} %wd_hbm.1, bf16[64,512]{1,0:T(8,128)(2,1)} %bitcast.12, bf16[64,512]{1,0:T(8,128)(2,1)} %bitcast.13, ...), custom_call_target="tpu_custom_call" | custom-call | tf_op jit(solution)/shard_map/pallas_call | solution.py:654
  69.8 1.4 %copy.15 = f32[4,2048]{1,0:T(4,128)} copy(f32[4,2048]{1,0:T(4,128)} %shard_map.127) | data formatting | bytes 65536
